TPU v7x, 32 devices: a whole 2x2x4 slice. The times are simulated.
32 devices in a mesh: groups: 2 (over x), tile: 16 (over z, y, core).
Axes of the slice: x: 2, y: 2, z: 4, core: 2. Of those that a mesh axis runs over, the one named last changes fastest.
Arguments:
- features: bfloat16 [2, 192, 160, 256], P('groups', 'tile'), parts along dimension 0, may hold values from -6 to 6
- cotangent: bfloat16 [2, 192, 160, 256], P('groups', 'tile'), parts along dimension 0, may hold values from -6 to 6
- weight_one: bfloat16 [256, 9, 256], replicated, may hold values from -0.125 to 0.125
- weight_two: bfloat16 [256, 9, 256], replicated, may hold values from -0.125 to 0.125
Outputs:
- block_out: bfloat16 [2, 192, 160, 256], P('groups', 'tile'), parts along dimension 0
- input_grad: bfloat16 [2, 192, 160, 256], P('groups', 'tile'), parts along dimension 0
- grad_one: float32 [256, 18, 256], P('tile', 'groups'), parts along dimension 1
- grad_two: float32 [256, 18, 256], P('tile', 'groups'), parts along dimension 1
There are 2 independent parts, one for each index of `groups`. A program takes and returns all parts, laid end to end along the dimension named above; an argument that names none is the same for every part. Nothing has to cross between parts.
All inputs are finite; a program needn't handle non-finite values.
Results may differ from a plain program's by a relative error of at most 0.0032.
Values may be sent and summed in bfloat16 or wider, within the bound.
A program may use at most 128 MiB of HBM per device.

v0:
```python
import jax
import jax.numpy as jnp
from jax import lax
from jax.sharding import PartitionSpec as P


def extended_2(shard, sides, width):
    for axis, dim in sides:
        size, length = (lax.axis_size(axis), shard.shape[dim])
        up = [(i, (i + 1) % size) for i in range(size - 1)]
        down = [(j, i) for i, j in up]
        last = lax.slice_in_dim(shard, length - width, length, axis=dim)
        leading = lax.slice_in_dim(shard, 0, width, axis=dim)
        before = lax.ppermute(last, axis, up)
        after = lax.ppermute(leading, axis, down)
        shard = jnp.concatenate([before, shard, after], axis=dim)
    return shard


def pad_columns(field):
    return jnp.pad(field, ((0, 0), (0, 0), (1, 1), (0, 0)))


def band_forward(extended, kernel, row_count):
    col_count = extended.shape[2] - 2
    total = jnp.zeros((extended.shape[0], row_count, col_count, kernel.shape[2]), jnp.float32)
    for tap_index in range(9):
        row_shift = tap_index // 3 - 1
        col_shift = tap_index % 3 - 1
        piece = extended[
            :,
            1 + row_shift : 1 + row_shift + row_count,
            1 + col_shift : 1 + col_shift + col_count,
            :,
        ]
        total = total + jnp.einsum(
            "brwi,io->brwo", piece, kernel[:, tap_index, :], preferred_element_type=jnp.float32
        )
    return total


def band_transpose(extended, kernel, row_count):
    col_count = extended.shape[2] - 2
    total = jnp.zeros((extended.shape[0], row_count, col_count, kernel.shape[0]), jnp.float32)
    for tap_index in range(9):
        row_shift = tap_index // 3 - 1
        col_shift = tap_index % 3 - 1
        piece = extended[
            :,
            1 - row_shift : 1 - row_shift + row_count,
            1 - col_shift : 1 - col_shift + col_count,
            :,
        ]
        total = total + jnp.einsum(
            "brwo,io->brwi", piece, kernel[:, tap_index, :], preferred_element_type=jnp.float32
        )
    return total


def kernel_term(extended, grad, scale):
    row_count = grad.shape[1]
    col_count = grad.shape[2]
    taps = []
    for tap_index in range(9):
        row_shift = tap_index // 3 - 1
        col_shift = tap_index % 3 - 1
        piece = extended[
            :,
            1 + row_shift : 1 + row_shift + row_count,
            1 + col_shift : 1 + col_shift + col_count,
            :,
        ]
        taps.append(jnp.einsum("brwi,brwo->io", piece, grad, preferred_element_type=jnp.float32))
    return jnp.stack(taps, axis=1) * scale


def body(features, cotangent, weight_one, weight_two):
    batch_count, row_count, col_count, channel_count = features.shape
    tile_count = lax.axis_size("tile")
    scale = float(batch_count * row_count * tile_count * col_count) ** (-0.5)
    input_deep = pad_columns(extended_2(features, (("tile", 1),), 2))
    pre_ext = band_forward(input_deep, weight_one, row_count + 2)
    global_row = lax.axis_index("tile") * row_count + jnp.arange(row_count + 2, dtype=jnp.int32) - 1
    inside = (global_row >= 0) & (global_row < row_count * tile_count)
    hidden_wide = jnp.where(inside[None, :, None, None], jax.nn.silu(pre_ext), 0.0).astype(
        jnp.bfloat16
    )
    hidden_ext = pad_columns(hidden_wide)
    pre = pre_ext[:, 1 : row_count + 1]
    input_ext = input_deep[:, 1 : row_count + 3]
    block_out = (
        features.astype(jnp.float32) + band_forward(hidden_ext, weight_two, row_count)
    ).astype(jnp.bfloat16)
    cot_ext = pad_columns(extended_2(cotangent, (("tile", 1),), 1))
    hidden_grad = band_transpose(cot_ext, weight_two, row_count)
    sigma = jax.nn.sigmoid(pre)
    slope = (hidden_grad * sigma * (1.0 + pre * (1.0 - sigma))).astype(jnp.bfloat16)
    slope_ext = pad_columns(extended_2(slope, (("tile", 1),), 1))
    input_grad = (
        cotangent.astype(jnp.float32) + band_transpose(slope_ext, weight_one, row_count)
    ).astype(jnp.bfloat16)
    term_one = kernel_term(input_ext, slope, scale)
    term_two = kernel_term(hidden_ext, cotangent, scale)
    grad_one, grad_two = (
        lax.psum_scatter(term_one, "tile", scatter_dimension=0, tiled=True),
        lax.psum_scatter(term_two, "tile", scatter_dimension=0, tiled=True),
    )
    return (block_out, input_grad, grad_one, grad_two)


def solution(mesh):
    in_specs = (P("groups", "tile", None, None), P("groups", "tile", None, None), P(), P())
    out_specs = (
        P("groups", "tile", None, None),
        P("groups", "tile", None, None),
        P("tile", "groups", None),
        P("tile", "groups", None),
    )
    return jax.shard_map(body, mesh=mesh, in_specs=in_specs, out_specs=out_specs, check_vma=False)
```

profile of v0, /device:TPU:0, one launch (start us, length us, event | category | flops | bytes accessed | tf_op | source)
XLA Modules:
  0.0 191.0 jit_solution(103128488341649687)
XLA Ops:
  7.2 1.1 fusion.249
  8.3 2.4 %collective-permute-start = (bf16[1,2,160,256]{3,2,1,0:T(8,128)(2,1)S(1)}, bf16[1,2,160,256]{3,2,1,0:T(8,128)(2,1)S(1)}, u32[]{:S(2)}, u32[]{:S(2)}) collective-permute-start(bf16[1,2,160,256]{3,2,1,0:T(8,128)(2,1)S(1)} %get-tuple-element.11), channel_id=1, source_target_pairs={{0,1},{1,2},{2,3},{3,4},{4,5},{5,6},{6,7},{7,8},{8,9},{9,10},{10,1... | collective-permute-start | bytes 491528 | tf_op jit(solution)/shard_map/ppermute | solution.py:14
  10.7 1.3 collective-permute-start.1
  12.0 0.9 fusion.248
  12.9 5.2 %collective-permute-start.2 = (bf16[1,1,160,256]{3,2,1,0:T(8,128)(2,1)S(1)}, bf16[1,1,160,256]{3,2,1,0:T(8,128)(2,1)S(1)}, u32[]{:S(2)}, u32[]{:S(2)}) collective-permute-start(bf16[1,1,160,256]{3,2,1,0:T(8,128)(2,1)S(1)} %get-tuple-element.6), channel_id=1, source_target_pairs={{0,1},{1,2},{2,3},{3,4},{4,5},{5,6},{6,7},{7,8},{8,9},{9,10},{10,1... | collective-permute-start | bytes 245768 | tf_op jit(solution)/shard_map/ppermute | solution.py:14
  18.1 1.3 collective-permute-start.3
  19.4 2.7 %fusion.107 = f32[12,160,256]{2,1,0:T(8,128)} fusion(bf16[1,12,160,256]{3,2,1,0:T(8,128)(2,1)S(1)} %copy-done, bf16[256,9,256]{2,0,1:T(8,128)(2,1)} %param.7), kind=kOutput, calls=%fused_computation.152 | convolution fusion | flops 251658240 | bytes 3080192 | tf_op jit(solution)/shard_map/brwo,io->brwi/dot_general | solution.py:54
  22.9 0.5 copy-done.9
  23.4 1.8 fusion.67
  25.1 1.8 fusion.71
  27.0 1.8 fusion.72
  28.7 1.8 fusion.73
  30.5 1.7 fusion.74
  32.2 1.8 fusion.79
  34.0 1.7 fusion.76
  36.1 1.1 copy-done.7
  37.6 0.5 fusion.35
  38.1 0.5 fusion.37
  38.6 0.5 fusion.39
  39.1 0.5 fusion.41
  39.6 0.5 fusion.45
  41.0 1.2 add_add_fusion
  42.2 0.7 fusion.53
  42.9 0.7 copy-done.3
  44.1 0.5 fusion.17
  44.5 0.5 fusion.16
  45.0 0.5 fusion.15
  45.5 0.5 fusion.14
  46.0 0.5 fusion.13
  46.5 0.5 fusion.12
  47.0 0.5 fusion.11
  47.5 0.5 fusion.10
  48.0 1.7 broadcast_multiply_fusion
  50.0 6.9 %fusion.3 = bf16[1,12,160,256]{3,2,1,0:T(8,128)(2,1)S(1)} fusion(f32[1,14,160,256]{3,2,1,0:T(8,128)} %bitcast.406, f32[12,160,256]{2,1,0:T(8,128)} %fusion.67, f32[12,160,256]{2,1,0:T(8,128)} %fusion.71, f32[12,160,256]{2,1,0:T(8,128)} %fusion.72, f32[12,160,256]{2,1,0:T(8,128)} %fusion.107, f32[12,160,256]{2,1,0:T(8,128)} %fusion.73, ...), kind=kOutput, calls=%fused_computation.9 | convolution fusion | flops 260505600 | bytes 19873792 | tf_op jit(solution)/shard_map/brwo,io->brwi/dot_general | solution.py:54
  56.9 0.5 fusion.27
  57.4 1.1 copy-done.14
  58.5 0.5 fusion.26
  59.0 0.5 fusion.25
  59.5 0.5 fusion.24
  60.0 0.7 copy-done.5
  60.7 0.5 fusion.23
  61.3 0.5 fusion.22
  61.8 0.7 fusion.247
  62.4 1.3 collective-permute-start.5
  63.7 6.0 %collective-permute-start.4 = (bf16[1,1,160,256]{3,2,1,0:T(8,128)(2,1)}, bf16[1,1,160,256]{3,2,1,0:T(8,128)(2,1)}, u32[]{:S(2)}, u32[]{:S(2)}) collective-permute-start(bf16[1,1,160,256]{3,2,1,0:T(8,128)(2,1)} %get-tuple-element.4), channel_id=1, source_target_pairs={{0,1},{1,2},{2,3},{3,4},{4,5},{5,6},{6,7},{7,8},{8,9},{9,10},{10,1... | collective-permute-start | bytes 245768 | tf_op jit(solution)/shard_map/ppermute | solution.py:14
  69.7 0.5 fusion.21
  70.2 0.5 fusion.20
  70.7 0.5 fusion.19
  71.2 0.8 copy-done.10
  72.0 1.8 fusion.112
  73.8 1.7 fusion.115
  75.6 1.7 fusion.118
  77.3 1.7 fusion.121
  79.0 1.7 fusion.124
  80.7 1.7 fusion.132
  82.4 1.7 fusion.133
  84.1 1.7 fusion.134
  85.8 1.6 broadcast_multiply_fusion.1
  87.5 1.2 copy-done.6
  88.7 7.8 %fusion.4 = bf16[1,12,160,256]{3,2,1,0:T(8,128)(2,1)} fusion(f32[12,160,256]{2,1,0:T(8,128)} %fusion.134, f32[12,160,256]{2,1,0:T(8,128)} %fusion.112, f32[12,160,256]{2,1,0:T(8,128)} %fusion.115, f32[12,160,256]{2,1,0:T(8,128)} %fusion.133, f32[12,160,256]{2,1,0:T(8,128)} %fusion.118, f32[12,160,256]{2,1,0:T(8,128)} %fusion.121, ...), kind=kOutput, calls=%fused_computation.11 | convolution fusion | flops 257064960 | bytes 18972672 | tf_op jit(solution)/shard_map/brwi,io->brwo/dot_general | solution.py:36
  97.0 1.2 select_maximum_fusion
  101.4 3.0 %fusion.1 = bf16[1,12,160,256]{3,2,1,0:T(8,128)(2,1)} fusion(f32[12,160,256]{2,1,0:T(8,128)S(1)} %fusion.54, f32[12,160,256]{2,1,0:T(8,128)S(1)} %fusion.58, f32[12,160,256]{2,1,0:T(8,128)S(1)} %fusion.59, f32[12,160,256]{2,1,0:T(8,128)S(1)} %fusion.96, f32[12,160,256]{2,1,0:T(8,128)S(1)} %fusion.60, f32[12,160,256]{2,1,0:T(8,128)S(1)} %fusion.61, ...), kind=kOutput, calls=%fused_computation.6 | convolution fusion | flops 257556480 | bytes 18890752 | tf_op jit(solution)/shard_map/brwo,io->brwi/dot_general | solution.py:54
  104.4 13.0 %reduce-scatter.5.cloned.1.call-done = f32[16,9,256]{2,0,1:T(8,128)} async-done(((f32[256,9,256]{2,0,1:T(8,128)}), f32[16,9,256]{2,0,1:T(8,128)}) %reduce-scatter.5.cloned.1.call-update) | async-done | bytes 147472 | tf_op jit(solution)/shard_map/reduce_scatter | solution.py:106
  117.4 66.8 %reduce-scatter.3.cloned.1.call-done = f32[16,9,256]{2,0,1:T(8,128)} async-done(((f32[256,9,256]{2,0,1:T(8,128)}), f32[16,9,256]{2,0,1:T(8,128)}) %reduce-scatter.3.cloned.1.call-update) | async-done | bytes 147472 | tf_op jit(solution)/shard_map/reduce_scatter | solution.py:105
  (50 shorter events, 6.9 us)
Async XLA Ops:
  7.2 12.2 %copy-start = (bf16[1,12,160,256]{3,2,1,0:T(8,128)(2,1)S(1)}, bf16[1,12,160,256]{3,2,1,0:T(8,128)(2,1)}, u32[]{:S(2)}) copy-start(bf16[1,12,160,256]{3,2,1,0:T(8,128)(2,1)} %param.5) | copy-start | bytes 2949124
  7.2 110.2 %reduce-scatter.5.cloned.1.call-start = ((), (), s32[]{:S(2)}) async-start(), calls=%async_computation.3 | async-start | bytes 2506752 | tf_op jit(solution)/shard_map/reduce_scatter | solution.py:106
  8.3 27.4 %collective-permute-start = (bf16[1,2,160,256]{3,2,1,0:T(8,128)(2,1)S(1)}, bf16[1,2,160,256]{3,2,1,0:T(8,128)(2,1)S(1)}, u32[]{:S(2)}, u32[]{:S(2)}) collective-permute-start(bf16[1,2,160,256]{3,2,1,0:T(8,128)(2,1)S(1)} %get-tuple-element.11), channel_id=1, source_target_pairs={{0,1},{1,2},{2,3},{3,4},{4,5},{5,6},{6,7},{7,8},{8,9},{9,10},{10,1... | collective-permute-start | bytes 491528 | tf_op jit(solution)/shard_map/ppermute | solution.py:14
  10.7 25.4 %collective-permute-start.1 = (bf16[1,2,160,256]{3,2,1,0:T(8,128)(2,1)S(1)}, bf16[1,2,160,256]{3,2,1,0:T(8,128)(2,1)S(1)}, u32[]{:S(2)}, u32[]{:S(2)}) collective-permute-start(bf16[1,2,160,256]{3,2,1,0:T(8,128)(2,1)S(1)} %get-tuple-element.12), channel_id=1, source_target_pairs={{1,0},{2,1},{3,2},{4,3},{5,4},{6,5},{7,6},{8,7},{9,8},{10,9},{11,1... | collective-permute-start | bytes 491528 | tf_op jit(solution)/shard_map/ppermute | solution.py:15
  12.9 9.2 %collective-permute-start.2 = (bf16[1,1,160,256]{3,2,1,0:T(8,128)(2,1)S(1)}, bf16[1,1,160,256]{3,2,1,0:T(8,128)(2,1)S(1)}, u32[]{:S(2)}, u32[]{:S(2)}) collective-permute-start(bf16[1,1,160,256]{3,2,1,0:T(8,128)(2,1)S(1)} %get-tuple-element.6), channel_id=1, source_target_pairs={{0,1},{1,2},{2,3},{3,4},{4,5},{5,6},{6,7},{7,8},{8,9},{9,10},{10,1... | collective-permute-start | bytes 245768 | tf_op jit(solution)/shard_map/ppermute | solution.py:14
  18.1 4.4 %collective-permute-start.3 = (bf16[1,1,160,256]{3,2,1,0:T(8,128)(2,1)S(1)}, bf16[1,1,160,256]{3,2,1,0:T(8,128)(2,1)S(1)}, u32[]{:S(2)}, u32[]{:S(2)}) collective-permute-start(bf16[1,1,160,256]{3,2,1,0:T(8,128)(2,1)S(1)} %get-tuple-element.7), channel_id=1, source_target_pairs={{1,0},{2,1},{3,2},{4,3},{5,4},{6,5},{7,6},{8,7},{9,8},{10,9},{11,1... | collective-permute-start | bytes 245768 | tf_op jit(solution)/shard_map/ppermute | solution.py:15
  22.1 1.3 copy-start.9
  34.0 1.7 copy-start.4
  35.8 1.4 copy-start.7
  36.0 4.5 %copy-start.13 = (bf16[1,14,160,256]{3,2,1,0:T(8,128)(2,1)}, bf16[1,14,160,256]{3,2,1,0:T(8,128)(2,1)S(1)}, u32[]{:S(2)}) copy-start(bf16[1,14,160,256]{3,2,1,0:T(8,128)(2,1)S(1)} %get-tuple-element.8) | copy-start | bytes 3440644
  36.1 4.0 %copy-start.11 = (bf16[1,14,160,256]{3,2,1,0:T(8,128)(2,1)}, bf16[1,14,160,256]{3,2,1,0:T(8,128)(2,1)S(1)}, u32[]{:S(2)}) copy-start(bf16[1,14,160,256]{3,2,1,0:T(8,128)(2,1)S(1)} %get-tuple-element.16) | copy-start | bytes 3440644
  42.2 1.4 copy-start.3
  49.8 134.4 %reduce-scatter.3.cloned.1.call-start = ((), (), s32[]{:S(2)}) async-start(), calls=%async_computation.2 | async-start | bytes 2506752 | tf_op jit(solution)/shard_map/reduce_scatter | solution.py:105
  56.9 13.8 %copy-start.1 = (bf16[1,12,160,256]{3,2,1,0:T(8,128)(2,1)}, bf16[1,12,160,256]{3,2,1,0:T(8,128)(2,1)S(1)}, u32[]{:S(2)}) copy-start(bf16[1,12,160,256]{3,2,1,0:T(8,128)(2,1)S(1)} %fusion.3) | copy-start | bytes 2949124
  56.9 1.6 copy-start.14
  59.5 1.2 copy-start.5
  62.4 34.5 %collective-permute-start.5 = (bf16[1,1,160,256]{3,2,1,0:T(8,128)(2,1)}, bf16[1,1,160,256]{3,2,1,0:T(8,128)(2,1)S(1)}, u32[]{:S(2)}, u32[]{:S(2)}) collective-permute-start(bf16[1,1,160,256]{3,2,1,0:T(8,128)(2,1)} %get-tuple-element.5), channel_id=1, source_target_pairs={{1,0},{2,1},{3,2},{4,3},{5,4},{6,5},{7,6},{8,7},{9,8},{10,9},{11,1... | collective-permute-start | bytes 245768 | tf_op jit(solution)/shard_map/ppermute | solution.py:15
  63.7 6.5 %copy-start.12 = (bf16[1,14,160,256]{3,2,1,0:T(8,128)(2,1)S(1)}, bf16[1,14,160,256]{3,2,1,0:T(8,128)(2,1)}, u32[]{:S(2)}) copy-start(bf16[1,14,160,256]{3,2,1,0:T(8,128)(2,1)} %copy-done.11) | copy-start | bytes 3440644
  63.7 33.2 %collective-permute-start.4 = (bf16[1,1,160,256]{3,2,1,0:T(8,128)(2,1)}, bf16[1,1,160,256]{3,2,1,0:T(8,128)(2,1)}, u32[]{:S(2)}, u32[]{:S(2)}) collective-permute-start(bf16[1,1,160,256]{3,2,1,0:T(8,128)(2,1)} %get-tuple-element.4), channel_id=1, source_target_pairs={{0,1},{1,2},{2,3},{3,4},{4,5},{5,6},{6,7},{7,8},{8,9},{9,10},{10,1... | collective-permute-start | bytes 245768 | tf_op jit(solution)/shard_map/ppermute | solution.py:14
  70.7 1.3 copy-start.10
  87.5 1.2 copy-start.6
  88.7 7.8 %copy-start.2 = (bf16[1,12,160,256]{3,2,1,0:T(8,128)(2,1)S(1)}, bf16[1,12,160,256]{3,2,1,0:T(8,128)(2,1)}, u32[]{:S(2)}) copy-start(bf16[1,12,160,256]{3,2,1,0:T(8,128)(2,1)} %copy-done.1) | copy-start | bytes 2949124
  88.7 7.8 %copy-start.8 = (bf16[256,9,256]{2,0,1:T(8,128)(2,1)S(1)}, bf16[256,9,256]{2,0,1:T(8,128)(2,1)}, u32[]{:S(2)}) copy-start(bf16[256,9,256]{2,0,1:T(8,128)(2,1)} %param.6) | copy-start | bytes 3538948
Sparse Core Ops, SparseCore 0:
  49.9 67.4 reduce-scatter.4
  122.2 61.9 reduce-scatter.2
where the time goes:
time: 192 us; the launch traced here: 191 us
  waiting for transfers between devices  80.2 us (42%)
  matrix products  63.9 us (33%)
  starting transfers between devices  17.6 us (9%)
  between operations  14.5 us (8%)
  local copies, waits for them, and re-layouts  9.13 us (5%)
  other arithmetic  5.66 us (3%)
    reduce_scatter x1, waiting for transfers between devices, body(): lax.psum_scatter(term_one, 'tile', scatter_dimension=0, tiled=True)  66.8 us
    dot_general x18, matrix products, band_transpose(): jnp.einsum('brwo,io->brwi', piece, kernel[:, tap_index, :], preferred_ele...  28.5 us
    dot_general x18, matrix products, band_forward(): jnp.einsum('brwi,io->brwo', piece, kernel[:, tap_index, :], preferred_ele...  26.6 us
    ppermute x3, starting transfers between devices, extended_2(): before = lax.ppermute(last, axis, up)  13.5 us
    reduce_scatter x1, waiting for transfers between devices, body(): lax.psum_scatter(term_two, 'tile', scatter_dimension=0, tiled=True)  13 us
    dot_general x18, matrix products, kernel_term(): jnp.einsum('brwi,brwo->io', piece, grad, preferred_element_type=jnp.float32)  8.8 us
    unnamed x31, local copies, waits for them, and re-layouts  6.14 us
    ppermute x3, starting transfers between devices, extended_2(): after = lax.ppermute(leading, axis, down)  3.86 us
  transfers between devices with their start and end apart: 8, of which 3 were waited for; matrix products, arithmetic and copies ran while one was open for 31% of the time, Pallas kernels for 0%

commit v1 on v0

v1 whole, which is shorter than its diff:
```python
import functools

import jax
import jax.numpy as jnp
from jax import lax
from jax.experimental import pallas as pl
from jax.experimental.pallas import tpu as pltpu
from jax.sharding import PartitionSpec as P

MESH = pl.DeviceIdType.MESH


def reversed_bits(value, width):
    out = 0
    for _ in range(width):
        out, value = out * 2 + value % 2, value // 2
    return out


def kernel(
    n, rows, cols, scale,
    x_ref, c_ref, before_ref, after_ref, w1_ref, w1t_ref, w2_ref, w2t_ref,
    out_ref, ingrad_ref, g_ref,
    sx, sc, sh, ss, deriv, acc, sent, got, send_sem, recv_sem,
):
    ch = x_ref.shape[1]
    stages = n.bit_length() - 1
    rc = ch // n
    me = lax.axis_index("tile")

    def bit_of(k):
        return (me // (1 << k)) % 2

    def partner_of(k):
        return me + (1 - 2 * bit_of(k)) * (1 << k)

    barrier = pltpu.get_barrier_semaphore()
    for k in range(stages):
        pl.semaphore_signal(barrier, inc=1, device_id={"tile": partner_of(k)}, device_id_type=MESH)

    def start_of(k):
        at = 0
        for m in range(k):
            at = at + bit_of(m) * (n >> (m + 1))
        return at

    def copy_of(g, k):
        half, off = n >> (k + 1), n - (n >> k)
        return pltpu.make_async_remote_copy(
            src_ref=sent.at[g, pl.ds(off, half)],
            dst_ref=got.at[g, pl.ds(off, half)],
            send_sem=send_sem.at[g, k],
            recv_sem=recv_sem.at[g, k],
            device_id={"tile": partner_of(k)},
            device_id_type=MESH,
        )

    def send(g, k):
        half, off = n >> (k + 1), n - (n >> k)
        base = start_of(k) + (1 - bit_of(k)) * half

        def step(p, carry):
            sent[g, off + p] = acc[g, base + p].astype(jnp.bfloat16)
            return carry

        lax.fori_loop(0, half, step, 0)
        copy_of(g, k).start()

    def receive(g, k):
        half, off = n >> (k + 1), n - (n >> k)
        base = start_of(k + 1)
        copy_of(g, k).wait()

        def step(p, carry):
            acc[g, base + p] = acc[g, base + p] + got[g, off + p].astype(jnp.float32)
            return carry

        lax.fori_loop(0, half, step, 0)

    def advance(g, k):
        receive(g, k)
        if k + 1 < stages:
            send(g, k + 1)
        else:
            g_ref[g] = acc[g, start_of(stages)]

    column = lax.broadcasted_iota(jnp.int32, (cols, ch), 0)

    def put_sides(dst, at, row):
        wide = row.astype(jnp.float32)
        left = jnp.where(column == 0, 0.0, pltpu.roll(wide, 1, 0))
        right = jnp.where(column == cols - 1, 0.0, pltpu.roll(wide, cols - 1, 0))
        dst[pl.ds(at, cols), 0:ch] = left.astype(jnp.bfloat16)
        dst[pl.ds(at, cols), 2 * ch : 3 * ch] = right.astype(jnp.bfloat16)

    def put(dst, at, row):
        dst[pl.ds(at, cols), ch : 2 * ch] = row
        put_sides(dst, at, row)

    def fill(dst, src, place):
        for r in range(2):
            put(dst, r * cols, before_ref[place + r])
            put(dst, (rows + 2 + r) * cols, after_ref[place + r])

        def step(r, carry):
            at = pl.multiple_of(r * cols, cols)
            put(dst, at + 2 * cols, src[pl.ds(at, cols), :])
            return carry

        lax.fori_loop(0, rows, step, 0)

    def fill_sides(dst):
        def step(r, carry):
            at = pl.multiple_of(r * cols, cols)
            put_sides(dst, at, dst[pl.ds(at, cols), ch : 2 * ch])
            return carry

        lax.fori_loop(0, rows + 2, step, 0)

    def conv(src, at, count, weight):
        total = None
        for a in range(3):
            term = jnp.dot(
                src[(at + a) * cols : (at + a + count) * cols, :],
                weight[a],
                preferred_element_type=jnp.float32,
            )
            total = term if total is None else total + term
        return total

    def kernel_term(g, left, src, at):
        for a in range(3):
            term = scale * jnp.dot(
                left,
                src[(at + a) * cols : (at + a + rows) * cols, :],
                preferred_element_type=jnp.float32,
            )
            for j in range(3):
                for chunk in range(n):
                    acc[g, reversed_bits(chunk, stages), 8 - (3 * a + j)] = term[
                        chunk * rc : (chunk + 1) * rc, j * ch : (j + 1) * ch
                    ]

    half_ext, half_own = (rows + 2) // 2, rows // 2
    top = jnp.where(me == 0, 0.0, 1.0)
    bottom = jnp.where(me == n - 1, 0.0, 1.0)

    fill(sx, x_ref, 0)
    for part in range(2):
        count = half_ext if part == 0 else rows + 2 - half_ext
        lo = part * half_ext
        pre = conv(sx, lo, count, w1_ref)
        sig = 1.0 / (1.0 + jnp.exp(-pre))
        hid = (pre * sig).astype(jnp.bfloat16)
        sh[lo * cols : (lo + count) * cols, ch : 2 * ch] = hid
        deriv[lo * cols : (lo + count) * cols, :] = sig * (1.0 + pre * (1.0 - sig))
    last = (rows + 1) * cols
    for at, keep in ((0, top), (last, bottom)):
        edge = sh[at : at + cols, ch : 2 * ch].astype(jnp.float32) * keep
        sh[at : at + cols, ch : 2 * ch] = edge.astype(jnp.bfloat16)
        deriv[at : at + cols, :] = deriv[at : at + cols, :] * keep

    fill(sc, c_ref, 2)
    kernel_term(1, sh[cols : (rows + 1) * cols, ch : 2 * ch].T, sc, 1)
    pl.semaphore_wait(barrier, stages)
    send(1, 0)

    for part in range(2):
        count = half_ext if part == 0 else rows + 2 - half_ext
        lo = part * half_ext
        grad = conv(sc, lo, count, w2t_ref)
        ss[lo * cols : (lo + count) * cols, ch : 2 * ch] = (
            grad * deriv[lo * cols : (lo + count) * cols, :]
        ).astype(jnp.bfloat16)
        if part == 0:
            advance(1, 0)
    fill_sides(ss)
    kernel_term(0, x_ref[...].T, ss, 0)
    send(0, 0)
    if stages > 1:
        advance(1, 1)

    fill_sides(sh)
    done = {0: 0, 1: min(2, stages)}

    def move(g):
        if done[g] < stages:
            advance(g, done[g])
            done[g] += 1

    for part in range(2):
        rs = slice(part * half_own * cols, (part + 1) * half_own * cols)
        total = conv(sh, part * half_own, half_own, w2_ref)
        out_ref[rs, :] = (x_ref[rs, :].astype(jnp.float32) + total).astype(jnp.bfloat16)
        move(0)
        move(1)
    for part in range(2):
        rs = slice(part * half_own * cols, (part + 1) * half_own * cols)
        total = conv(ss, part * half_own, half_own, w1t_ref)
        ingrad_ref[rs, :] = (c_ref[rs, :].astype(jnp.float32) + total).astype(jnp.bfloat16)
        move(0)
        move(1)
    for _ in range(stages):
        move(1)
        move(0)


def body(features, cotangent, weight_one, weight_two):
    batch, rows, cols, ch = features.shape
    n = lax.axis_size("tile")
    stages = n.bit_length() - 1
    scale = float(batch * rows * n * cols) ** (-0.5)
    up = [(i, i + 1) for i in range(n - 1)]
    down = [(j, i) for i, j in up]
    x, c = features[0], cotangent[0]
    before = lax.ppermute(jnp.concatenate([x[-2:], c[-2:]]), "tile", up)
    after = lax.ppermute(jnp.concatenate([x[:2], c[:2]]), "tile", down)

    def straight(w):
        return jnp.transpose(w, (1, 0, 2)).reshape(3, 3 * ch, ch)

    def turned(w):
        return jnp.flip(jnp.transpose(w, (1, 2, 0)), 0).reshape(3, 3 * ch, ch)

    flat = (rows * cols, ch)
    rc = ch // n
    bf, f32 = jnp.bfloat16, jnp.float32
    vm = pl.BlockSpec(memory_space=pltpu.VMEM)
    out, ingrad, grads = pl.pallas_call(
        functools.partial(kernel, n, rows, cols, scale),
        out_shape=(
            jax.ShapeDtypeStruct(flat, bf),
            jax.ShapeDtypeStruct(flat, bf),
            jax.ShapeDtypeStruct((2, 9, rc, ch), f32),
        ),
        in_specs=[vm] * 8,
        out_specs=(vm, vm, vm),
        scratch_shapes=[
            pltpu.VMEM(((rows + 4) * cols, 3 * ch), bf),
            pltpu.VMEM(((rows + 4) * cols, 3 * ch), bf),
            pltpu.VMEM(((rows + 2) * cols, 3 * ch), bf),
            pltpu.VMEM(((rows + 2) * cols, 3 * ch), bf),
            pltpu.VMEM(((rows + 2) * cols, ch), f32),
            pltpu.VMEM((2, n, 9, rc, ch), f32),
            pltpu.VMEM((2, n - 1, 9, rc, ch), bf),
            pltpu.VMEM((2, n - 1, 9, rc, ch), bf),
            pltpu.SemaphoreType.DMA((2, stages)),
            pltpu.SemaphoreType.DMA((2, stages)),
        ],
        compiler_params=pltpu.CompilerParams(
            collective_id=0, has_side_effects=True, vmem_limit_bytes=56 * 1024 * 1024
        ),
        cost_estimate=pl.CostEstimate(
            flops=6 * 18 * rows * cols * ch * ch, bytes_accessed=16 * 1024 * 1024, transcendentals=rows * cols * ch
        ),
    )(
        x.reshape(flat), c.reshape(flat), before, after,
        straight(weight_one), turned(weight_one), straight(weight_two), turned(weight_two),
    )
    grads = jnp.transpose(grads, (0, 2, 1, 3))
    return (out.reshape(features.shape), ingrad.reshape(features.shape), grads[0], grads[1])


def solution(mesh):
    in_specs = (P("groups", "tile", None, None), P("groups", "tile", None, None), P(), P())
    out_specs = (
        P("groups", "tile", None, None),
        P("groups", "tile", None, None),
        P("tile", "groups", None),
        P("tile", "groups", None),
    )
    return jax.shard_map(body, mesh=mesh, in_specs=in_specs, out_specs=out_specs, check_vma=False)
```

time: 192 us -> 67.9 us (0.35)
  waiting for transfers between devices: 80.2 us -> 0.61 us
  matrix products: 63.9 us -> 0 us
  Pallas kernels: 0 us -> 50.9 us
  between operations: 14.5 us -> 0.7 us
  starting transfers between devices: 17.6 us -> 4.37 us
  other arithmetic: 5.66 us -> 1.51 us
    reduce_scatter x2 -> x0, waiting for transfers between devices: 79.8 us -> none  [the longest x1 66.8 us: body(): lax.psum_scatter(term_one, 'tile', scatter_dimension=0, tiled=True)]
    dot_general x54 -> x0, matrix products: 63.9 us -> none  [the longest x18 28.5 us: band_transpose(): jnp.einsum('brwo,io->brwi', piece, kernel[:, tap_index, :], preferred_ele...]
    pallas_call x0 -> x1, Pallas kernels: none -> 50.9 us  [body(): pl.pallas_call(functools.partial(kernel, n, rows, cols, scale), out_shape...]
    ppermute x6 -> x2, starting transfers between devices: 17.3 us -> 4.37 us  [the longest x1 3.09 us: body(): before = lax.ppermute(jnp.concatenate([x[-2:], c[-2:]]), 'tile', up)]
    mul x2 -> x0, other arithmetic: 3.36 us -> none  [kernel_term(): return jnp.stack(taps, axis=1) * scale]
    rev x0 -> x4, local copies, waits for them, and re-layouts: none -> 3.32 us  [turned(): return jnp.flip(jnp.transpose(w, (1, 2, 0)), 0).reshape(3, 3 * ch, ch)]
    unnamed x31 -> x8, local copies, waits for them, and re-layouts: 6.14 us -> 3.17 us
  transfers between devices with their start and end apart: 8 -> 2, of which waited for: 3 -> 1; matrix products, arithmetic and copies ran while one was open for 31% -> 6% of each run, Pallas kernels for 0% -> 0%
where the time goes in v1:
time: 67.9 us; the launch traced here: 67.6 us
  Pallas kernels  50.9 us (75%)
  local copies, waits for them, and re-layouts  9.57 us (14%)
  starting transfers between devices  4.37 us (6%)
  other arithmetic  1.51 us (2%)
  between operations  0.7 us (1%)
    pallas_call x1, Pallas kernels, body(): pl.pallas_call(functools.partial(kernel, n, rows, cols, scale), out_shape...  50.9 us
    rev x4, local copies, waits for them, and re-layouts, turned(): return jnp.flip(jnp.transpose(w, (1, 2, 0)), 0).reshape(3, 3 * ch, ch)  3.32 us
    unnamed x8, local copies, waits for them, and re-layouts  3.17 us
    ppermute x1, starting transfers between devices, body(): before = lax.ppermute(jnp.concatenate([x[-2:], c[-2:]]), 'tile', up)  3.09 us
    squeeze x1, local copies, waits for them, and re-layouts, body(): grads[1]  1.8 us
  transfers between devices with their start and end apart: 2, of which 1 were waited for; matrix products, arithmetic and copies ran while one was open for 6% of the time, Pallas kernels for 0%

profile of v1, /device:TPU:0, one launch (start us, length us, event | category | flops | bytes accessed | tf_op | source)
XLA Modules:
  0.0 67.6 jit_solution(15531293549626735125)
XLA Ops:
  0.6 0.0 copy-start.1
  0.6 1.3 %slice_bitcast_fusion = (bf16[2,160,256]{2,1,0:T(8,128)(2,1)S(1)}, bf16[2,160,256]{2,1,0:T(8,128)(2,1)S(1)}, bf16[2,160,256]{2,1,0:T(8,128)(2,1)S(1)}, bf16[2,160,256]{2,1,0:T(8,128)(2,1)S(1)}) fusion(bf16[1,12,160,256]{3,2,1,0:T(8,128)(2,1)} %param.5, bf16[1,12,160,256]{3,2,1,0:T(8,128)(2,1)} %param.4), kind=kLoop, calls=%fused_computation.2 | loop fusion | bytes 1310720 | tf_op jit(solution)/shard_map/slice | solution.py:217
  1.9 0.8 %pad_maximum_fusion = bf16[4,160,256]{2,1,0:T(8,128)(2,1)} fusion(bf16[2,160,256]{2,1,0:T(8,128)(2,1)S(1)} %get-tuple-element.13, bf16[2,160,256]{2,1,0:T(8,128)(2,1)S(1)} %get-tuple-element.16), kind=kLoop, calls=%fused_computation | loop fusion | flops 163840 | bytes 655360 | tf_op jit(solution)/shard_map/concatenate | solution.py:216
  2.7 3.1 %collective-permute-start = (bf16[4,160,256]{2,1,0:T(8,128)(2,1)}, bf16[4,160,256]{2,1,0:T(8,128)(2,1)}, u32[]{:S(2)}, u32[]{:S(2)}) collective-permute-start(bf16[4,160,256]{2,1,0:T(8,128)(2,1)} %pad_maximum_fusion), channel_id=1, source_target_pairs={{0,1},{1,2},{2,3},{3,4},{4,5},{5,6},{6,7},{7,8},{8,9},{9,10},{10,1... | collective-permute-start | bytes 983048 | tf_op jit(solution)/shard_map/ppermute | solution.py:216
  5.8 0.8 %pad_maximum_fusion.1 = bf16[4,160,256]{2,1,0:T(8,128)(2,1)} fusion(bf16[2,160,256]{2,1,0:T(8,128)(2,1)S(1)} %get-tuple-element.12, bf16[2,160,256]{2,1,0:T(8,128)(2,1)S(1)} %get-tuple-element.17), kind=kLoop, calls=%fused_computation.1 | loop fusion | flops 163840 | bytes 655360 | tf_op jit(solution)/shard_map/concatenate | solution.py:217
  6.5 1.3 %collective-permute-start.1 = (bf16[4,160,256]{2,1,0:T(8,128)(2,1)}, bf16[4,160,256]{2,1,0:T(8,128)(2,1)}, u32[]{:S(2)}, u32[]{:S(2)}) collective-permute-start(bf16[4,160,256]{2,1,0:T(8,128)(2,1)} %pad_maximum_fusion.1), channel_id=1, source_target_pairs={{1,0},{2,1},{3,2},{4,3},{5,4},{6,5},{7,6},{8,7},{9,8},{10,9},{11,1... | collective-permute-start | bytes 983048 | tf_op jit(solution)/shard_map/ppermute | solution.py:217
  7.8 0.0 copy-done.1
  7.8 0.1 rev.8
  7.9 0.0 copy-start
  7.9 1.6 %copy.9 = bf16[9,256,256]{2,1,0:T(8,128)(2,1)} copy(bf16[9,256,256]{1,2,0:T(8,128)(2,1)S(1)} %rev.8) | data formatting | bytes 2359296 | tf_op jit(solution)/shard_map/jit(_flip)/rev | solution.py:223
  9.5 0.0 copy-done
  9.5 0.1 rev.7
  9.6 1.6 %copy.8 = bf16[9,256,256]{2,1,0:T(8,128)(2,1)} copy(bf16[9,256,256]{1,2,0:T(8,128)(2,1)S(1)} %rev.7) | data formatting | bytes 2359296 | tf_op jit(solution)/shard_map/jit(_flip)/rev | solution.py:223
  11.2 0.0 collective-permute-done.before_ref
  11.2 0.6 collective-permute-done.1.after_ref
  11.8 50.9 %shard_map.75 = (bf16[1920,256]{1,0:T(8,128)(2,1)}, bf16[1920,256]{1,0:T(8,128)(2,1)}, f32[2,9,16,256]{3,2,1,0:T(8,128)}) custom-call(bf16[1920,256]{1,0:T(8,128)(2,1)} %bitcast.36, bf16[1920,256]{1,0:T(8,128)(2,1)} %bitcast.37, bf16[4,160,256]{2,1,0:T(8,128)(2,1)} %collective-permute-done.before_ref, bf16[4,160,256]{2,1,0:T(8,128)(2,1)} %collective-permute-done.1.after_ref, ...), custom_call_target="tpu_custom_call" | custom-call | flops 13589544960 | bytes 16777216 | tf_op jit(solution)/shard_map/pallas_call | solution.py:229
  62.7 0.0 copy-start.2
  62.7 1.8 %slice_bitcast_fusion.4 = (f32[16,9,256]{2,0,1:T(8,128)}, f32[16,9,256]{2,0,1:T(8,128)}) fusion(f32[2,16,9,256]{3,1,2,0:T(8,128)} %bitcast.35), kind=kLoop, calls=%fused_computation.6 | loop fusion | bytes 589824 | tf_op jit(solution)/shard_map/squeeze | solution.py:261
  64.5 2.2 %copy.12 = bf16[1,12,160,256]{3,2,1,0:T(8,128)(2,1)} copy(bf16[1,12,160,256]{3,2,1,0:T(8,128)(2,1)} %bitcast.34) | data formatting | bytes 1966080
  66.7 0.0 copy-done.2
  66.7 0.9 %copy.13 = bf16[1,12,160,256]{3,2,1,0:T(8,128)(2,1)} copy(bf16[1,12,160,256]{3,2,1,0:T(8,128)(2,1)S(1)} %bitcast.33) | data formatting | bytes 1966080
Async XLA Ops:
  0.6 7.2 %copy-start.1 = (bf16[256,9,256]{2,0,1:T(8,128)(2,1)S(1)}, bf16[256,9,256]{2,0,1:T(8,128)(2,1)}, u32[]{:S(2)}) copy-start(bf16[256,9,256]{2,0,1:T(8,128)(2,1)} %param.7) | copy-start | bytes 3538948
  2.7 8.5 %collective-permute-start = (bf16[4,160,256]{2,1,0:T(8,128)(2,1)}, bf16[4,160,256]{2,1,0:T(8,128)(2,1)}, u32[]{:S(2)}, u32[]{:S(2)}) collective-permute-start(bf16[4,160,256]{2,1,0:T(8,128)(2,1)} %pad_maximum_fusion), channel_id=1, source_target_pairs={{0,1},{1,2},{2,3},{3,4},{4,5},{5,6},{6,7},{7,8},{8,9},{9,10},{10,1... | collective-permute-start | bytes 983048 | tf_op jit(solution)/shard_map/ppermute | solution.py:216
  6.5 5.3 %collective-permute-start.1 = (bf16[4,160,256]{2,1,0:T(8,128)(2,1)}, bf16[4,160,256]{2,1,0:T(8,128)(2,1)}, u32[]{:S(2)}, u32[]{:S(2)}) collective-permute-start(bf16[4,160,256]{2,1,0:T(8,128)(2,1)} %pad_maximum_fusion.1), channel_id=1, source_target_pairs={{1,0},{2,1},{3,2},{4,3},{5,4},{6,5},{7,6},{8,7},{9,8},{10,9},{11,1... | collective-permute-start | bytes 983048 | tf_op jit(solution)/shard_map/ppermute | solution.py:217
  7.9 1.6 %copy-start = (bf16[256,9,256]{2,0,1:T(8,128)(2,1)S(1)}, bf16[256,9,256]{2,0,1:T(8,128)(2,1)}, u32[]{:S(2)}) copy-start(bf16[256,9,256]{2,0,1:T(8,128)(2,1)} %param.6) | copy-start | bytes 3538948
  62.7 4.0 %copy-start.2 = (bf16[1920,256]{1,0:T(8,128)(2,1)S(1)}, bf16[1920,256]{1,0:T(8,128)(2,1)}, u32[]{:S(2)}) copy-start(bf16[1920,256]{1,0:T(8,128)(2,1)} %get-tuple-element.8) | copy-start | bytes 2949124

commit v2 on v1

v2 whole, which is shorter than its diff:
```python
import functools

import jax
import jax.numpy as jnp
from jax import lax
from jax.experimental import pallas as pl
from jax.experimental.pallas import tpu as pltpu
from jax.sharding import PartitionSpec as P

MESH = pl.DeviceIdType.MESH


def position(chunk, order):
    out = 0
    for bit in order:
        out = out * 2 + (chunk >> bit) % 2
    return out


def kernel(
    n, rows, cols, scale,
    x_ref, c_ref, w1_ref, w2_ref,
    out_ref, ingrad_ref, g1_ref, g2_ref,
    w1t_ref, w2t_ref, sx, sc, sh, ss, deriv, before_ref, after_ref, acc, got_wide, sent, got,
    edge_send, edge_recv, send_sem, recv_sem,
):
    ch = x_ref.shape[1]
    stages = n.bit_length() - 1
    rc = ch // n
    me = lax.axis_index("tile")
    plain = list(range(stages))
    turned = plain[:1] + plain[2:] + plain[1:2]
    orders = (plain, turned, plain)

    def bit_of(bit):
        return (me // (1 << bit)) % 2

    def partner_of(bit):
        return me + (1 - 2 * bit_of(bit)) * (1 << bit)

    barrier = pltpu.get_barrier_semaphore()
    for k in range(stages):
        pl.semaphore_signal(barrier, inc=1, device_id={"tile": partner_of(k)}, device_id_type=MESH)

    @pl.when(me > 0)
    def _():
        pl.semaphore_signal(barrier, inc=1, device_id={"tile": me - 1}, device_id_type=MESH)

    @pl.when(me < n - 1)
    def _():
        pl.semaphore_signal(barrier, inc=1, device_id={"tile": me + 1}, device_id_type=MESH)

    neighbours = jnp.where(me > 0, 1, 0) + jnp.where(me < n - 1, 1, 0)
    pl.semaphore_wait(barrier, stages + neighbours)

    two = 2 * cols

    def edge_up(f):
        src = (x_ref, c_ref)[f]
        return pltpu.make_async_remote_copy(
            src_ref=src.at[pl.ds((rows - 2) * cols, two)],
            dst_ref=before_ref.at[f],
            send_sem=edge_send.at[0, f],
            recv_sem=edge_recv.at[0, f],
            device_id={"tile": me + 1},
            device_id_type=MESH,
        )

    def edge_down(f):
        src = (x_ref, c_ref)[f]
        return pltpu.make_async_remote_copy(
            src_ref=src.at[pl.ds(0, two)],
            dst_ref=after_ref.at[f],
            send_sem=edge_send.at[1, f],
            recv_sem=edge_recv.at[1, f],
            device_id={"tile": me - 1},
            device_id_type=MESH,
        )

    for f in range(2):
        @pl.when(me < n - 1)
        def _():
            edge_up(f).start()

        @pl.when(me > 0)
        def _():
            edge_down(f).start()

    def edges_arrive(f):
        @pl.when(me > 0)
        def _():
            edge_up(f).wait_recv()

        @pl.when(me < n - 1)
        def _():
            edge_down(f).wait_recv()

        @pl.when(me == 0)
        def _():
            before_ref[f] = jnp.zeros((two, ch), jnp.bfloat16)

        @pl.when(me == n - 1)
        def _():
            after_ref[f] = jnp.zeros((two, ch), jnp.bfloat16)

    def start_of(a, k):
        at = 0
        for m in range(k):
            at = at + bit_of(orders[a][m]) * (n >> (m + 1))
        return at

    def copy_of(g, a, k):
        half, off = n >> (k + 1), n // 2 - (n >> k)
        if k == 0:
            src = acc.at[g, a, pl.ds((1 - bit_of(orders[a][0])) * half, half)]
            dst = got_wide.at[g, a]
        else:
            src = sent.at[g, a, pl.ds(off, half)]
            dst = got.at[g, a, pl.ds(off, half)]
        return pltpu.make_async_remote_copy(
            src_ref=src,
            dst_ref=dst,
            send_sem=send_sem.at[g, a, k],
            recv_sem=recv_sem.at[g, a, k],
            device_id={"tile": partner_of(orders[a][k])},
            device_id_type=MESH,
        )

    def send(g, a, k):
        half, off = n >> (k + 1), n // 2 - (n >> k)
        if k > 0:
            base = start_of(a, k) + (1 - bit_of(orders[a][k])) * half

            def step(p, carry):
                sent[g, a, off + p] = acc[g, a, base + p].astype(jnp.bfloat16)
                return carry

            lax.fori_loop(0, half, step, 0)
        copy_of(g, a, k).start()

    def receive(g, a, k):
        half, off = n >> (k + 1), n // 2 - (n >> k)
        base = start_of(a, k + 1)
        copy_of(g, a, k).wait()

        def step(p, carry):
            term = got_wide[g, a, p] if k == 0 else got[g, a, off + p].astype(jnp.float32)
            acc[g, a, base + p] = acc[g, a, base + p] + term
            return carry

        lax.fori_loop(0, half, step, 0)

    done = {}

    def move(g):
        for a in range(3):
            k = done[g, a]
            if k < stages:
                receive(g, a, k)
                done[g, a] = k + 1
                if k + 1 < stages:
                    send(g, a, k + 1)
                else:
                    last = acc[g, a, start_of(a, stages)]
                    for j in range(3):
                        (g1_ref, g2_ref)[g][8 - (3 * a + j)] = last[j]

    column = lax.broadcasted_iota(jnp.int32, (cols, ch), 0)

    def put_sides(dst, at, row):
        wide = row.astype(jnp.float32)
        left = jnp.where(column == 0, 0.0, pltpu.roll(wide, 1, 0))
        right = jnp.where(column == cols - 1, 0.0, pltpu.roll(wide, cols - 1, 0))
        dst[pl.ds(at, cols), 0:ch] = left.astype(jnp.bfloat16)
        dst[pl.ds(at, cols), 2 * ch : 3 * ch] = right.astype(jnp.bfloat16)

    def put(dst, at, row):
        dst[pl.ds(at, cols), ch : 2 * ch] = row
        put_sides(dst, at, row)

    def fill(dst, src, place):
        def step(r, carry):
            at = pl.multiple_of(r * cols, cols)
            put(dst, at + 2 * cols, src[pl.ds(at, cols), :])
            return carry

        lax.fori_loop(0, rows, step, 0)
        edges_arrive(place)
        for r in range(2):
            put(dst, r * cols, before_ref[place, r * cols : (r + 1) * cols, :])
            put(dst, (rows + 2 + r) * cols, after_ref[place, r * cols : (r + 1) * cols, :])

    def fill_sides(dst):
        def step(r, carry):
            at = pl.multiple_of(r * cols, cols)
            put_sides(dst, at, dst[pl.ds(at, cols), ch : 2 * ch])
            return carry

        lax.fori_loop(0, rows + 2, step, 0)

    def conv(src, at, count, weight):
        total = None
        for a in range(3):
            term = jnp.dot(
                src[(at + a) * cols : (at + a + count) * cols, :],
                weight[a],
                preferred_element_type=jnp.float32,
            )
            total = term if total is None else total + term
        return total

    def kernel_term(g, left, src, at, between=None):
        for a in range(3):
            term = scale * jnp.dot(
                left,
                src[(at + a) * cols : (at + a + rows) * cols, :],
                preferred_element_type=jnp.float32,
            )
            for j in range(3):
                for chunk in range(n):
                    acc[g, a, position(chunk, orders[a]), j] = term[
                        chunk * rc : (chunk + 1) * rc, j * ch : (j + 1) * ch
                    ]
            send(g, a, 0)
            done[g, a] = 0
            if between is not None and a == 1:
                between()

    half_ext, half_own = (rows + 2) // 2, rows // 2
    top = jnp.where(me == 0, 0.0, 1.0)
    bottom = jnp.where(me == n - 1, 0.0, 1.0)

    for dst, src in ((w2t_ref, w2_ref), (w1t_ref, w1_ref)):
        for a in range(3):
            for j in range(3):
                dst[a, j * ch : (j + 1) * ch, :] = src[2 - a, (2 - j) * ch : (3 - j) * ch, :].T

    fill(sx, x_ref, 0)
    for part in range(2):
        count = half_ext if part == 0 else rows + 2 - half_ext
        lo = part * half_ext
        pre = conv(sx, lo, count, w1_ref)
        sig = 1.0 / (1.0 + jnp.exp(-pre))
        hid = (pre * sig).astype(jnp.bfloat16)
        sh[lo * cols : (lo + count) * cols, ch : 2 * ch] = hid
        deriv[lo * cols : (lo + count) * cols, :] = sig * (1.0 + pre * (1.0 - sig))
    last = (rows + 1) * cols
    for at, keep in ((0, top), (last, bottom)):
        edge = sh[at : at + cols, ch : 2 * ch].astype(jnp.float32) * keep
        sh[at : at + cols, ch : 2 * ch] = edge.astype(jnp.bfloat16)
        deriv[at : at + cols, :] = deriv[at : at + cols, :] * keep

    fill(sc, c_ref, 1)
    kernel_term(1, sh[cols : (rows + 1) * cols, ch : 2 * ch].T, sc, 1)

    for part in range(2):
        count = half_ext if part == 0 else rows + 2 - half_ext
        lo = part * half_ext
        grad = conv(sc, lo, count, w2t_ref)
        ss[lo * cols : (lo + count) * cols, ch : 2 * ch] = (
            grad * deriv[lo * cols : (lo + count) * cols, :]
        ).astype(jnp.bfloat16)
        if part == 0:
            move(1)
    fill_sides(ss)
    kernel_term(0, x_ref[...].T, ss, 0, lambda: move(1))

    fill_sides(sh)
    move(0)
    for part in range(2):
        rs = slice(part * half_own * cols, (part + 1) * half_own * cols)
        total = conv(sh, part * half_own, half_own, w2_ref)
        out_ref[rs, :] = (x_ref[rs, :].astype(jnp.float32) + total).astype(jnp.bfloat16)
        move(1 - part)
    for part in range(2):
        rs = slice(part * half_own * cols, (part + 1) * half_own * cols)
        total = conv(ss, part * half_own, half_own, w1t_ref)
        ingrad_ref[rs, :] = (c_ref[rs, :].astype(jnp.float32) + total).astype(jnp.bfloat16)
        move(1 - part)
    for _ in range(stages):
        move(0)
        move(1)
    for f in range(2):
        @pl.when(me < n - 1)
        def _():
            edge_up(f).wait_send()

        @pl.when(me > 0)
        def _():
            edge_down(f).wait_send()


def body(features, cotangent, weight_one, weight_two):
    batch, rows, cols, ch = features.shape
    n = lax.axis_size("tile")
    stages = n.bit_length() - 1
    scale = float(batch * rows * n * cols) ** (-0.5)
    x, c = features[0], cotangent[0]

    def straight(w):
        return jnp.transpose(w, (1, 0, 2)).reshape(3, 3 * ch, ch)

    flat = (rows * cols, ch)
    rc = ch // n
    bf, f32 = jnp.bfloat16, jnp.float32
    vm = pl.BlockSpec(memory_space=pltpu.VMEM)
    out, ingrad, grad_one, grad_two = pl.pallas_call(
        functools.partial(kernel, n, rows, cols, scale),
        out_shape=(
            jax.ShapeDtypeStruct(flat, bf),
            jax.ShapeDtypeStruct(flat, bf),
            jax.ShapeDtypeStruct((9, rc, ch), f32),
            jax.ShapeDtypeStruct((9, rc, ch), f32),
        ),
        in_specs=[vm] * 4,
        out_specs=(vm, vm, vm, vm),
        scratch_shapes=[
            pltpu.VMEM((3, 3 * ch, ch), bf),
            pltpu.VMEM((3, 3 * ch, ch), bf),
            pltpu.VMEM(((rows + 4) * cols, 3 * ch), bf),
            pltpu.VMEM(((rows + 4) * cols, 3 * ch), bf),
            pltpu.VMEM(((rows + 2) * cols, 3 * ch), bf),
            pltpu.VMEM(((rows + 2) * cols, 3 * ch), bf),
            pltpu.VMEM(((rows + 2) * cols, ch), f32),
            pltpu.VMEM((2, 2 * cols, ch), bf),
            pltpu.VMEM((2, 2 * cols, ch), bf),
            pltpu.VMEM((2, 3, n, 3, rc, ch), f32),
            pltpu.VMEM((2, 3, n // 2, 3, rc, ch), f32),
            pltpu.VMEM((2, 3, max(n // 2 - 1, 1), 3, rc, ch), bf),
            pltpu.VMEM((2, 3, max(n // 2 - 1, 1), 3, rc, ch), bf),
            pltpu.SemaphoreType.DMA((2, 2)),
            pltpu.SemaphoreType.DMA((2, 2)),
            pltpu.SemaphoreType.DMA((2, 3, stages)),
            pltpu.SemaphoreType.DMA((2, 3, stages)),
        ],
        compiler_params=pltpu.CompilerParams(
            collective_id=0, has_side_effects=True, vmem_limit_bytes=56 * 1024 * 1024
        ),
        cost_estimate=pl.CostEstimate(
            flops=6 * 18 * rows * cols * ch * ch, bytes_accessed=16 * 1024 * 1024, transcendentals=rows * cols * ch
        ),
    )(
        x.reshape(flat), c.reshape(flat),
        straight(weight_one), straight(weight_two),
    )
    return (out.reshape(features.shape), ingrad.reshape(features.shape), jnp.transpose(grad_one, (1, 0, 2)), jnp.transpose(grad_two, (1, 0, 2)))


def solution(mesh):
    in_specs = (P("groups", "tile", None, None), P("groups", "tile", None, None), P(), P())
    out_specs = (
        P("groups", "tile", None, None),
        P("groups", "tile", None, None),
        P("tile", "groups", None),
        P("tile", "groups", None),
    )
    return jax.shard_map(body, mesh=mesh, in_specs=in_specs, out_specs=out_specs, check_vma=False)
```

time: 67.9 us -> 56 us (0.82)
  local copies, waits for them, and re-layouts: 9.57 us -> 4.65 us
  starting transfers between devices: 4.37 us -> 0 us
  other arithmetic: 1.51 us -> 0 us
    ppermute x2 -> x0, starting transfers between devices: 4.37 us -> none  [the longest x1 3.09 us: body(): before = lax.ppermute(jnp.concatenate([x[-2:], c[-2:]]), 'tile', up)]
    rev x4 -> x0, local copies, waits for them, and re-layouts: 3.32 us -> none  [turned(): return jnp.flip(jnp.transpose(w, (1, 2, 0)), 0).reshape(3, 3 * ch, ch)]
    squeeze x1 -> x0, local copies, waits for them, and re-layouts: 1.8 us -> none  [body(): grads[1]]
    concatenate x2 -> x0, other arithmetic: 1.51 us -> none  [the longest x1 0.75 us: body(): before = lax.ppermute(jnp.concatenate([x[-2:], c[-2:]]), 'tile', up)]
    unnamed x8 -> x10, local copies, waits for them, and re-layouts: 3.17 us -> 4.65 us
    slice x1 -> x0, local copies, waits for them, and re-layouts: 1.29 us -> none  [body(): after = lax.ppermute(jnp.concatenate([x[:2], c[:2]]), 'tile', down)]
  transfers between devices with their start and end apart: 2 -> 0, of which waited for: 1 -> 0; matrix products, arithmetic and copies ran while one was open for 6% -> 0% of each run, Pallas kernels for 0% -> 0%
where the time goes in v2:
time: 56 us; the launch traced here: 55.8 us
  Pallas kernels  50.5 us (90%)
  local copies, waits for them, and re-layouts  4.65 us (8%)
  between operations  0.65 us (1%)
    pallas_call x1, Pallas kernels, body(): pl.pallas_call(functools.partial(kernel, n, rows, cols, scale), out_shape...  50.5 us
    unnamed x10, local copies, waits for them, and re-layouts  4.65 us

profile of v2, /device:TPU:0, one launch (start us, length us, event | category | flops | bytes accessed | tf_op | source)
XLA Modules:
  0.0 55.8 jit_solution(585398790165288927)
XLA Ops:
  0.6 50.5 %shard_map.75 = (bf16[1920,256]{1,0:T(8,128)(2,1)}, bf16[1920,256]{1,0:T(8,128)(2,1)}, f32[9,16,256]{2,1,0:T(8,128)}, f32[9,16,256]{2,1,0:T(8,128)}) custom-call(bf16[1920,256]{1,0:T(8,128)(2,1)} %bitcast.18, bf16[1920,256]{1,0:T(8,128)(2,1)} %bitcast.19, bf16[3,768,256]{2,1,0:T(8,128)(2,1)} %bitcast.16, bf16[3,768,256]{2,1,0:T(8,128)(2,1)} %bitcast.17), custom_call_target="tpu_custom_call" | custom-call | flops 13589544960 | bytes 16777216 | tf_op jit(solution)/shard_map/pallas_call | solution.py:307
  51.1 0.0 copy-start
  51.1 2.3 %copy.12 = bf16[1,12,160,256]{3,2,1,0:T(8,128)(2,1)} copy(bf16[1,12,160,256]{3,2,1,0:T(8,128)(2,1)} %bitcast.13) | data formatting | bytes 1966080
  53.4 0.0 copy-done
  53.4 0.0 copy-start.2
  53.4 0.0 copy-start.1
  53.4 0.9 %copy.13 = bf16[1,12,160,256]{3,2,1,0:T(8,128)(2,1)} copy(bf16[1,12,160,256]{3,2,1,0:T(8,128)(2,1)S(1)} %bitcast.12) | data formatting | bytes 1966080
  54.4 0.1 copy-done.2
  54.5 0.7 %copy.14 = f32[16,9,256]{2,0,1:T(8,128)} copy(f32[16,9,256]{2,0,1:T(8,128)S(1)} %bitcast.15) | data formatting | bytes 294912
  55.1 0.0 copy-done.1
  55.1 0.7 %copy.15 = f32[16,9,256]{2,0,1:T(8,128)} copy(f32[16,9,256]{2,0,1:T(8,128)S(1)} %bitcast.14) | data formatting | bytes 294912
Async XLA Ops:
  51.1 2.3 %copy-start = (bf16[1920,256]{1,0:T(8,128)(2,1)S(1)}, bf16[1920,256]{1,0:T(8,128)(2,1)}, u32[]{:S(2)}) copy-start(bf16[1920,256]{1,0:T(8,128)(2,1)} %get-tuple-element.9) | copy-start | bytes 2949124
  53.4 1.0 %copy-start.2 = (f32[9,16,256]{2,1,0:T(8,128)S(1)}, f32[9,16,256]{2,1,0:T(8,128)}, u32[]{:S(2)}) copy-start(f32[9,16,256]{2,1,0:T(8,128)} %get-tuple-element.10) | copy-start | bytes 442372
  53.4 1.7 %copy-start.1 = (f32[9,16,256]{2,1,0:T(8,128)S(1)}, f32[9,16,256]{2,1,0:T(8,128)}, u32[]{:S(2)}) copy-start(f32[9,16,256]{2,1,0:T(8,128)} %get-tuple-element.11) | copy-start | bytes 442372

commit v3 on v2

--- a/solution.py
+++ b/solution.py
@@ -288,6 +288,21 @@
         @pl.when(me > 0)
         def _():
             edge_down(f).wait_send()
+
+
+def hand_on(pieces, a_in, b_in, c_in, d_in, a_out, b_out, c_out, d_out, sems):
+    copies = []
+    for src, dst in ((a_in, a_out), (b_in, b_out)):
+        size = src.shape[0] // pieces
+        for at in range(pieces):
+            rows = pl.ds(at * size, size)
+            copies.append((src.at[rows], dst.at[rows]))
+    copies += [(c_in, c_out), (d_in, d_out)]
+    started = [pltpu.make_async_copy(s, d, sems.at[i]) for i, (s, d) in enumerate(copies)]
+    for copy in started:
+        copy.start()
+    for copy in started:
+        copy.wait()
 
 
 def body(features, cotangent, weight_one, weight_two):
@@ -343,6 +358,17 @@
         x.reshape(flat), c.reshape(flat),
         straight(weight_one), straight(weight_two),
     )
+    anywhere = pl.BlockSpec(memory_space=pl.ANY)
+    results = (out, ingrad, grad_one, grad_two)
+    pieces = 4 if rows * cols % 64 == 0 else 1
+    out, ingrad, grad_one, grad_two = pl.pallas_call(
+        functools.partial(hand_on, pieces),
+        out_shape=tuple(jax.ShapeDtypeStruct(r.shape, r.dtype) for r in results),
+        in_specs=[anywhere] * 4,
+        out_specs=(anywhere,) * 4,
+        scratch_shapes=[pltpu.SemaphoreType.DMA((2 * pieces + 2,))],
+        compiler_params=pltpu.CompilerParams(vmem_limit_bytes=56 * 1024 * 1024),
+    )(*results)
     return (out.reshape(features.shape), ingrad.reshape(features.shape), jnp.transpose(grad_one, (1, 0, 2)), jnp.transpose(grad_two, (1, 0, 2)))
 
 

time: 56 us -> 121 us (2.16)
  Pallas kernels: 50.5 us -> 120 us
  local copies, waits for them, and re-layouts: 4.65 us -> 0 us
    pallas_call x0 -> x1, Pallas kernels: none -> 69.7 us  [body(): pl.pallas_call(functools.partial(hand_on, pieces), out_shape=tuple((jax.S...]
    unnamed x10 -> x0, local copies, waits for them, and re-layouts: 4.65 us -> none
where the time goes in v3:
time: 121 us
  Pallas kernels  120 us (99%)
    pallas_call x1, Pallas kernels, body(): pl.pallas_call(functools.partial(hand_on, pieces), out_shape=tuple((jax.S...  69.7 us
    pallas_call x1, Pallas kernels, body(): pl.pallas_call(functools.partial(kernel, n, rows, cols, scale), out_shape...  50.5 us

profile of v3, /device:TPU:0, one launch (start us, length us, event | category | flops | bytes accessed | tf_op | source)
XLA Modules:
  0.0 121.0 jit_solution(9933122215193160184)
XLA Ops:
  0.6 50.5 %shard_map.75 = (bf16[1920,256]{1,0:T(8,128)(2,1)}, bf16[1920,256]{1,0:T(8,128)(2,1)}, f32[9,16,256]{2,1,0:T(8,128)}, f32[9,16,256]{2,1,0:T(8,128)}) custom-call(bf16[1920,256]{1,0:T(8,128)(2,1)} %bitcast.14, bf16[1920,256]{1,0:T(8,128)(2,1)} %bitcast.15, bf16[3,768,256]{2,1,0:T(8,128)(2,1)} %bitcast.12, bf16[3,768,256]{2,1,0:T(8,128)(2,1)} %bitcast.13), custom_call_target="tpu_custom_call" | custom-call | flops 13589544960 | bytes 16777216 | tf_op jit(solution)/shard_map/pallas_call | solution.py:322
  51.1 69.7 %shard_map.76 = (bf16[1920,256]{1,0:T(8,128)(2,1)}, bf16[1920,256]{1,0:T(8,128)(2,1)}, f32[9,16,256]{2,1,0:T(8,128)}, f32[9,16,256]{2,1,0:T(8,128)}) custom-call(bf16[1920,256]{1,0:T(8,128)(2,1)} %get-tuple-element.12.a_in, bf16[1920,256]{1,0:T(8,128)(2,1)} %get-tuple-element.13.b_in, f32[9,16,256]{2,1,0:T(8,128)} %get-tuple-element.14.c_in, ...), custom_call_target="tpu_custom_call" | custom-call | tf_op jit(solution)/shard_map/pallas_call | solution.py:364
